TPU v7x, 32 devices: a whole 2x2x4 slice. The times are simulated.
32 devices in a mesh: grp: 2 (over x), seq: 16 (over z, y, core).
Axes of the slice: x: 2, y: 2, z: 4, core: 2. Of those that a mesh axis runs over, the one named last changes fastest.
Arguments:
- projected: bfloat16 [8192, 3, 1024], P(('grp', 'seq')), parts along dimension 0, may hold values from -6 to 6
- taps: float32 [3, 3, 1024], replicated, may hold values from -3.5 to 3.5
- filters: bfloat16 [1024, 4096], P('seq'), may hold values from -0.09375 to 0.09375
- skip: float32 [1024], P('seq'), may hold values from 0.5 to 1.5
Outputs:
- output: bfloat16 [8192, 1024], P(('grp', 'seq')), parts along dimension 0
There are 2 independent parts, one for each index of `grp`. A program takes and returns all parts, laid end to end along the dimension named above; an argument that names none is the same for every part. Nothing has to cross between parts.
All inputs are finite; a program needn't handle non-finite values.
Results may differ from a plain program's by a relative error of at most 0.009.
Values may be sent and summed in bfloat16 or wider, within the bound.
A program may use at most 64 MiB of HBM per device.

v0:
```python
import functools
import math

import jax
import jax.numpy as jnp
import numpy as np
from jax import lax
from jax.experimental import pallas as pl
from jax.experimental.pallas import tpu as pltpu
from jax.sharding import PartitionSpec as P

LANES = 128
SUB = 8
GROUP = 16
MAX_PHASES = 4
F32 = jnp.float32
BF16 = jnp.bfloat16


def factors(order):
    inner = 1 << ((int(math.log2(order)) + 1) // 2)
    return order // inner, inner


def dft_tables(order):
    n1, n2 = factors(order)
    half, hb = n1 // 2, n2 // 2
    groups = n2 // GROUP
    s = np.arange(half)[:, None, None]
    a = np.arange(half)[None, :, None]
    b = np.arange(n2)[None, None, :]
    theta = 2 * np.pi * ((s * (a * n2 + b)) % order) / order
    sign = np.broadcast_to((-1.0) ** np.arange(half)[:, None], (half, n2))
    fwd = np.stack((np.cos(theta), -np.sin(theta)), 1)
    fwd[0, 0] = 1.0
    fwd[0, 1] = sign
    inv = np.stack((2 * np.cos(theta), -2 * np.sin(theta)), 1)
    inv[0, 0] = 1.0
    inv[0, 1] = sign
    inv = inv / order
    eye = np.eye(GROUP)
    fwd_g = fwd.reshape(half, 2, half, groups, GROUP)
    first = np.einsum("srage,ef->gsreaf", fwd_g, eye).reshape(groups, 2 * half * GROUP, half * GROUP)
    inv_g = inv.reshape(half, 2, half, groups, GROUP)
    last = np.einsum("srage,ef->gaesrf", inv_g, eye).reshape(groups, half * GROUP, 2 * half * GROUP)
    k = np.arange(n2)
    phi = 2 * np.pi * (np.outer(k, k) % n2) / n2
    c, d = np.cos(phi), np.sin(phi)
    mid = np.block([[c, d], [-d, c]])
    back = np.block([[c, -d], [d, c]])
    kh = np.arange(hb)
    low = 2 * np.pi * (np.outer(kh, k) % n2) / n2
    odd = 2 * np.pi * (np.outer(half + n1 * kh, k) % order) / order
    mid0 = np.zeros((2 * n2, 2 * n2))
    mid0[:hb, :n2] = np.cos(low)
    mid0[hb:n2, n2:] = np.cos(odd)
    mid0[n2 : n2 + hb, :n2] = -np.sin(low)
    mid0[n2, :n2] = (-1.0) ** k
    mid0[n2 + hb :, n2:] = -np.sin(odd)
    back0 = 2 * mid0.T
    back0[:, 0] /= 2
    back0[:, n2] /= 2
    cast = lambda x: np.ascontiguousarray(x.astype(BF16))
    return cast(first), cast(np.stack((mid0, mid))), cast(np.stack((back0, back))), cast(last)


def plan(chans, lc, n):
    chunks = max(1, MAX_PHASES * lc // LANES)
    lc = lc // chunks
    return chunks, lc, LANES // lc


def kernel(
    n, chunks,
    proj_hbm, taps, filt_hbm, skip, first_hbm, mid_hbm, back_hbm, last_hbm,
    out,
    proj, filt, first, mid, back, last,
    margin, query, drive, pack, recv, tok, wide_f, spec_f, spec, done, ret,
    load, m_send, m_recv, send1, recv1, send2, recv2,
):
    me = lax.axis_index("seq")
    _, rows, chans = proj.shape
    count = taps.shape[0]
    lc = chans // n // chunks
    p = LANES // lc
    rpd = rows // p
    total = rpd * n
    n1, n2 = factors(2 * total)
    half = n1 // 2
    groups = n2 // GROUP
    tiles = chans // LANES
    own = p // chunks
    mrows = margin.shape[1]
    lane = lax.broadcasted_iota(jnp.int32, (1, LANES), 1) // lc

    loads = [
        pltpu.make_async_copy(a, b, load.at[k])
        for k, (a, b) in enumerate(
            ((proj_hbm, proj), (filt_hbm, filt.at[:, pl.ds(LANES, total * p)]), (first_hbm, first), (mid_hbm, mid), (back_hbm, back), (last_hbm, last))
        )
    ]
    for c in loads:
        c.start()

    barrier = pltpu.get_barrier_semaphore()

    @pl.loop(1, n)
    def _(i):
        pl.semaphore_signal(barrier, inc=1, device_id={"seq": lax.rem(me + i, n)})

    def lanes_of(tile):
        return pl.ds(pl.multiple_of(tile * LANES, LANES), LANES)

    def features(tile, ext, many):
        feats = []
        for m in range(3):
            x = ext(m)
            from_row = x.shape[0] - many
            acc = None
            for o in range(count):
                term = taps[o, m : m + 1, lanes_of(tile)] * x[from_row - o : from_row - o + many]
                acc = term if acc is None else acc + term
            feats.append(acc)
        return feats[0], (feats[1] * feats[2]).astype(BF16).astype(F32)

    def tile_features(tile):
        zero = jnp.zeros((SUB, LANES), F32)
        q, d = features(
            tile, lambda m: jnp.concatenate((zero, proj[m, :, lanes_of(tile)].astype(F32)), 0), rows
        )
        query[tile] = q
        drive[tile] = d

    loads[0].wait()
    pl.loop(0, tiles // 2)(tile_features)

    pl.semaphore_wait(barrier, n - 1)
    m_copy = pltpu.make_async_remote_copy(
        src_ref=proj.at[:, pl.ds(rows - mrows, mrows)],
        dst_ref=margin,
        send_sem=m_send,
        recv_sem=m_recv,
        device_id={"seq": lax.rem(me + 1, n)},
    )

    @pl.when(me < n - 1)
    def _():
        m_copy.start()

    pl.loop(tiles // 2, tiles)(tile_features)

    @pl.when(me > 0)
    def _():
        m_copy.wait_recv()

    @pl.when(me == 0)
    def _():
        margin[...] = jnp.zeros_like(margin)

    def block_rows(j):
        return pl.ds(pl.multiple_of(j * rpd, GROUP), rpd)

    def send_drive(k, i):
        dest = lax.rem(me + i, n)
        return pltpu.make_async_remote_copy(
            src_ref=pack.at[k, dest],
            dst_ref=recv.at[k, block_rows(me)],
            send_sem=send1.at[k, i],
            recv_sem=recv1.at[k, i],
            device_id={"seq": dest},
        )

    def send_long(k, i):
        dest = lax.rem(me + i, n)
        return pltpu.make_async_remote_copy(
            src_ref=done.at[k, block_rows(dest)],
            dst_ref=ret.at[k, me],
            send_sem=send2.at[k, i],
            recv_sem=recv2.at[k, i],
            device_id={"seq": dest},
        )

    @pl.loop(0, tiles, unroll=2)
    def _(step):
        tile = lax.rem(me // own + tiles // 2 + step, tiles)

        def ext(m):
            before = margin[m, :, lanes_of(tile)].astype(F32)
            after = proj[m, 0:16, lanes_of(tile)].astype(F32)
            return jnp.concatenate((before[mrows - SUB :], after[:SUB]), 0)

        q, dr = features(tile, ext, SUB)
        query[tile, 0:SUB] = q
        drive[tile, 0:SUB] = dr
        parts = [drive[tile, pl.ds(h, rpd, stride=p), :] for h in range(p)]
        for d in range(p):
            block = None
            for h in range(p):
                shift = ((h - d) % p) * lc
                moved = parts[h] if shift == 0 else pltpu.roll(parts[h], shift, 1)
                block = moved if block is None else jnp.where(lane == h, moved, block)
            block = block.astype(BF16)
            dest, k = tile * own + d // chunks, d % chunks

            @pl.when(dest == me)
            def _():
                recv[k, block_rows(me), :] = block

            @pl.when(dest != me)
            def _():
                pack[k, dest] = block
                if k == 0:
                    send_drive(k, lax.rem(dest - me + n, n)).start()

    for k in range(1, chunks):

        @pl.loop(0, n - 1)
        def _(step):
            i = lax.rem(n // 2 + step, n - 1) + 1
            send_drive(k, i).start()

    loads[1].wait()
    seg = LANES // p
    row_id = lax.broadcasted_iota(jnp.int32, (2 * LANES, 2 * LANES), 0)
    col_id = lax.broadcasted_iota(jnp.int32, (2 * LANES, 2 * LANES), 1)
    inside = lax.rem(row_id, LANES)
    source = LANES + p * lax.rem(inside, seg) + inside // seg - jnp.where(row_id < LANES, 0, p)
    apart = (col_id == source).astype(F32).astype(BF16)
    filt[:, 0:LANES] = jnp.zeros((filt.shape[0], LANES), BF16)

    @pl.loop(0, total // seg, unroll=4)
    def _(t):
        piece = filt[:, pl.ds(pl.multiple_of(t * LANES, LANES), 2 * LANES)]
        wide = jnp.concatenate([piece[k * lc : (k + 1) * lc] for k in range(chunks) for _ in range(p)], 0)
        turned = lax.dot_general(apart, wide, (((1,), (1,)), ((), ())), preferred_element_type=F32)
        at = pl.ds(pl.multiple_of(t * seg, GROUP), seg)
        for k in range(chunks):
            for b in range(p):
                now = turned[b * seg : (b + 1) * seg, k * LANES : (k + 1) * LANES]
                old = turned[LANES + b * seg : LANES + (b + 1) * seg, k * LANES : (k + 1) * LANES]
                tok[k, b, at, :] = jnp.where(lane < b, old, now).astype(BF16)

    for c in loads[2:]:
        c.wait()

    def group_rows(g, a=0):
        return pl.ds(pl.multiple_of(a * n2 + GROUP * g, GROUP), GROUP)

    def filter_spectrum(k):
        @pl.loop(0, groups, unroll=2)
        def _(g):
            wide = jnp.concatenate(
                [
                    jnp.concatenate([tok[k, b, group_rows(g, a), :] for a in range(half)], 0)
                    for b in range(p)
                ],
                1,
            )
            res = jnp.dot(first[g], wide, preferred_element_type=F32)
            wide_f[:, :, group_rows(g), :] = res.astype(BF16).reshape(half, 2, GROUP, p * LANES)

        def one(s, which):
            x = wide_f[s].reshape(2 * n2, p * LANES)
            z = jnp.dot(mid[which], x, preferred_element_type=F32)
            spec_f[s] = z.reshape(2, n2, p * LANES)

        one(0, 0)

        @pl.loop(1, half, unroll=5)
        def _(s):
            one(s, 1)

    def slabs(k, ss, which):
        x = jnp.concatenate([spec[s].reshape(2 * n2, LANES) for s in ss], 1)
        z = jnp.dot(mid[which], x, preferred_element_type=F32)
        ys = []
        for j, s in enumerate(ss):
            zr = z[:n2, j * LANES : (j + 1) * LANES]
            zi = z[n2:, j * LANES : (j + 1) * LANES]
            rr = ii = cross = None
            for b in range(p):
                xr = zr if b == 0 else pltpu.roll(zr, b * lc, 1)
                xi = zi if b == 0 else pltpu.roll(zi, b * lc, 1)
                gr = spec_f[s, 0, :, b * LANES : (b + 1) * LANES]
                gi = spec_f[s, 1, :, b * LANES : (b + 1) * LANES]
                add = lambda t, v: v if t is None else t + v
                rr = add(rr, xr * gr)
                ii = add(ii, xi * gi)
                cross = add(cross, xr * gi + xi * gr)
            if which == 0:
                top = lax.broadcasted_iota(jnp.int32, (n2, LANES), 0) == 0
                yr = jnp.where(top, rr, rr - ii)
                yi = jnp.where(top, ii, cross)
            else:
                yr, yi = rr - ii, cross
            ys.append(jnp.concatenate((yr, yi), 0).astype(BF16))
        v = jnp.dot(back[which], jnp.concatenate(ys, 1), preferred_element_type=F32)
        for j, s in enumerate(ss):
            spec[s] = v[:, j * LANES : (j + 1) * LANES].astype(BF16).reshape(2, n2, LANES)

    def convolve(k):
        @pl.loop(1, n)
        def _(i):
            send_drive(k, i).wait_recv()

        @pl.loop(0, groups, unroll=groups)
        def _(g):
            x = jnp.concatenate([recv[k, group_rows(g, a), :] for a in range(half)], 0)
            res = jnp.dot(first[g], x, preferred_element_type=F32)
            spec[:, :, group_rows(g), :] = res.astype(BF16).reshape(half, 2, GROUP, LANES)

        slabs(k, [0], 0)
        slabs(k, [1], 1)

        @pl.loop(1, half // 2, unroll=half // 2 - 1)
        def _(t):
            slabs(k, [2 * t, 2 * t + 1], 1)

        direct = jnp.concatenate([skip[:, k * lc : (k + 1) * lc]] * p, 1)

        @pl.loop(0, groups, unroll=groups)
        def _(g):
            v = spec[:, :, group_rows(g), :].reshape(2 * half * GROUP, LANES)
            y = jnp.dot(last[g], v, preferred_element_type=F32)
            for a in range(half):
                at = group_rows(g, a)
                both = y[a * GROUP : (a + 1) * GROUP] + direct * recv[k, at, :].astype(F32)
                done[k, at, :] = both.astype(BF16)

        ret[k, me] = done[k, block_rows(me), :]

        @pl.loop(0, n - 1)
        def _(step):
            send_long(k, lax.rem(n // 2 + step, n - 1) + 1).start()

    for k in range(chunks):
        filter_spectrum(k)
        convolve(k)

    @pl.when(me < n - 1)
    def _():
        m_copy.wait_send()

    for k in range(chunks):

        @pl.loop(1, n)
        def _(i):
            send_drive(k, i).wait_send()
            send_long(k, i).wait()

    @pl.loop(0, tiles, unroll=2)
    def _(tile):
        parts = [ret[d % chunks, tile * own + d // chunks].astype(F32) for d in range(p)]
        for h in range(p):
            block = None
            for d in range(p):
                shift = ((d - h) % p) * lc
                moved = parts[d] if shift == 0 else pltpu.roll(parts[d], shift, 1)
                block = moved if block is None else jnp.where(lane == d, moved, block)
            drive[tile, pl.ds(h, rpd, stride=p), :] = block
        out[:, lanes_of(tile)] = (query[tile] * drive[tile]).astype(BF16)


def body(n, projected, taps, filters, skip):
    rows, _, chans = projected.shape
    lc, length = filters.shape
    chunks, sc, p = plan(chans, lc, n)
    rpd = rows // p
    total = length // p
    n1, n2 = factors(2 * total)
    half = n1 // 2
    tables = [jnp.asarray(t) for t in dft_tables(2 * total)]
    vmem = pl.BlockSpec(memory_space=pltpu.VMEM)
    hbm = pl.BlockSpec(memory_space=pl.ANY)
    sems = pltpu.SemaphoreType.DMA((chunks, n))
    blocks = pltpu.VMEM((chunks, n, rpd, LANES), BF16)
    flat = pltpu.VMEM((chunks, total, LANES), BF16)
    moved = jnp.transpose(projected, (1, 0, 2))
    return pl.pallas_call(
        functools.partial(kernel, n, chunks),
        out_shape=jax.ShapeDtypeStruct((rows, chans), BF16),
        in_specs=[hbm, vmem, hbm, vmem] + [hbm] * 4,
        out_specs=vmem,
        scratch_shapes=[
            pltpu.VMEM(moved.shape, BF16),
            pltpu.VMEM((filters.shape[0], LANES + length), BF16),
            *[pltpu.VMEM(t.shape, BF16) for t in tables],
            pltpu.VMEM((3, 16, chans), BF16),
            pltpu.VMEM((chans // LANES, rows, LANES), F32),
            pltpu.VMEM((chans // LANES, rows, LANES), F32),
            blocks,
            flat,
            pltpu.VMEM((chunks, p, total, LANES), BF16),
            pltpu.VMEM((half, 2, n2, p * LANES), BF16),
            pltpu.VMEM((half, 2, n2, p * LANES), F32),
            pltpu.VMEM((half, 2, n2, LANES), BF16),
            flat,
            blocks,
            pltpu.SemaphoreType.DMA((6,)),
            pltpu.SemaphoreType.DMA,
            pltpu.SemaphoreType.DMA,
            sems, sems, sems, sems,
        ],
        compiler_params=pltpu.CompilerParams(
            collective_id=0, has_side_effects=True, vmem_limit_bytes=56 * 1024 * 1024
        ),
    )(moved, taps, filters, skip.reshape(1, lc), *tables)


def solution(mesh):
    placed = (P(("grp", "seq"), None, None), P(), P("seq", None), P("seq"))
    return jax.shard_map(
        functools.partial(body, mesh.shape["seq"]),
        mesh=mesh, in_specs=placed, out_specs=P(("grp", "seq"), None), check_vma=False,
    )
```

profile of v0, /device:TPU:0, one launch (start us, length us, event | category | flops | bytes accessed | tf_op | source)
XLA Modules:
  0.0 39.1 jit_solution(6522469681425188256)
XLA Ops:
  0.0 37.2 %shard_map.82 = bf16[256,1024]{1,0:T(8,128)(2,1)} custom-call(bf16[3,256,1024]{2,1,0:T(8,128)(2,1)} %bitcast.2, f32[3,3,1024]{2,1,0:T(4,128)} %taps.1, bf16[64,4096]{1,0:T(8,128)(2,1)} %filt_hbm.1, f32[1,64]{1,0:T(1,128)} %bitcast.3, bf16[4,512,256]{2,1,0:T(8,128)(2,1)} %constant.8.clone.first_hbm, bf16[2,128,128]{2,1,0:T(8,128)(2,1)} %constant.9.clone.mid_hbm, ...), custom_call_target="tpu_custom_call" | custom-call | tf_op jit(solution)/shard_map/pallas_call | solution.py:379
  37.2 1.9 %copy.10 = bf16[256,1024]{1,0:T(8,128)(2,1)} copy(bf16[256,1024]{1,0:T(8,128)(2,1)} %shard_map.82) | data formatting | bytes 1048576
where the time goes:
time: 39.3 us; the launch traced here: 39.1 us
  Pallas kernels  37.2 us (95%)
  local copies, waits for them, and re-layouts  1.87 us (5%)
    pallas_call x1, Pallas kernels, body(): pl.pallas_call(functools.partial(kernel, n, chunks), out_shape=jax.ShapeD...  37.2 us
    unnamed x1, local copies, waits for them, and re-layouts  1.87 us

commit v1 on v0

--- a/solution.py
+++ b/solution.py
@@ -123,7 +123,11 @@
             feats.append(acc)
         return feats[0], (feats[1] * feats[2]).astype(BF16).astype(F32)
 
-    def tile_features(tile):
+    def tile_at(step):
+        return lax.rem(me // own + tiles // 2 + step, tiles)
+
+    def tile_features(step):
+        tile = tile_at(step)
         zero = jnp.zeros((SUB, LANES), F32)
         q, d = features(
             tile, lambda m: jnp.concatenate((zero, proj[m, :, lanes_of(tile)].astype(F32)), 0), rows
@@ -147,7 +151,8 @@
     def _():
         m_copy.start()
 
-    pl.loop(tiles // 2, tiles)(tile_features)
+    early = 3 * tiles // 4
+    pl.loop(tiles // 2, early)(tile_features)
 
     @pl.when(me > 0)
     def _():
@@ -180,9 +185,8 @@
             device_id={"seq": dest},
         )
 
-    @pl.loop(0, tiles, unroll=2)
-    def _(step):
-        tile = lax.rem(me // own + tiles // 2 + step, tiles)
+    def send_tile(step):
+        tile = tile_at(step)
 
         def ext(m):
             before = margin[m, :, lanes_of(tile)].astype(F32)
@@ -212,12 +216,23 @@
                 if k == 0:
                     send_drive(k, lax.rem(dest - me + n, n)).start()
 
-    for k in range(1, chunks):
-
-        @pl.loop(0, n - 1)
-        def _(step):
-            i = lax.rem(n // 2 + step, n - 1) + 1
-            send_drive(k, i).start()
+    pl.loop(0, early, unroll=2)(send_tile)
+
+    @pl.loop(early, tiles)
+    def _(step):
+        tile_features(step)
+        send_tile(step)
+
+    def offset(step):
+        return lax.rem(n // 2 + step, n - 1) + 1
+
+    def follow(k, lo, hi):
+        if k + 1 < chunks:
+
+            @pl.loop(lo, hi)
+            def _(step):
+                send_drive(k, offset(step)).wait_send()
+                send_drive(k + 1, offset(step)).start()
 
     loads[1].wait()
     seg = LANES // p
@@ -247,6 +262,8 @@
         return pl.ds(pl.multiple_of(a * n2 + GROUP * g, GROUP), GROUP)
 
     def filter_spectrum(k):
+        follow(k, 0, n // 2)
+
         @pl.loop(0, groups, unroll=2)
         def _(g):
             wide = jnp.concatenate(
@@ -258,6 +275,8 @@
             )
             res = jnp.dot(first[g], wide, preferred_element_type=F32)
             wide_f[:, :, group_rows(g), :] = res.astype(BF16).reshape(half, 2, GROUP, p * LANES)
+
+        follow(k, n // 2, n - 1)
 
         def one(s, which):
             x = wide_f[s].reshape(2 * n2, p * LANES)
@@ -331,7 +350,7 @@
 
         @pl.loop(0, n - 1)
         def _(step):
-            send_long(k, lax.rem(n // 2 + step, n - 1) + 1).start()
+            send_long(k, offset(step)).start()
 
     for k in range(chunks):
         filter_spectrum(k)
@@ -341,15 +360,21 @@
     def _():
         m_copy.wait_send()
 
-    for k in range(chunks):
-
-        @pl.loop(1, n)
-        def _(i):
-            send_drive(k, i).wait_send()
-            send_long(k, i).wait()
-
-    @pl.loop(0, tiles, unroll=2)
-    def _(tile):
+    @pl.loop(1, n)
+    def _(i):
+        send_drive(chunks - 1, i).wait_send()
+
+    @pl.loop(0, tiles)
+    def _(step):
+        tile = lax.rem(me // own + tiles // 2 + tiles - step, tiles)
+        for d in range(own):
+            src = tile * own + d
+
+            @pl.when(src != me)
+            def _():
+                for k in range(chunks):
+                    send_long(k, lax.rem(me - src + n, n)).wait_recv()
+
         parts = [ret[d % chunks, tile * own + d // chunks].astype(F32) for d in range(p)]
         for h in range(p):
             block = None
@@ -359,6 +384,12 @@
                 block = moved if block is None else jnp.where(lane == d, moved, block)
             drive[tile, pl.ds(h, rpd, stride=p), :] = block
         out[:, lanes_of(tile)] = (query[tile] * drive[tile]).astype(BF16)
+
+    for k in range(chunks):
+
+        @pl.loop(1, n)
+        def _(i):
+            send_long(k, i).wait_send()
 
 
 def body(n, projected, taps, filters, skip):

time: 39.3 us -> 38.2 us (0.972)
  Pallas kernels: 37.2 us -> 36.2 us
    pallas_call x1, Pallas kernels: 37.2 us -> 36.2 us  [body(): pl.pallas_call(functools.partial(kernel, n, chunks), out_shape=jax.ShapeD...]
where the time goes in v1:
time: 38.2 us; the launch traced here: 38 us
  Pallas kernels  36.2 us (95%)
  local copies, waits for them, and re-layouts  1.87 us (5%)
    pallas_call x1, Pallas kernels, body(): pl.pallas_call(functools.partial(kernel, n, chunks), out_shape=jax.ShapeD...  36.2 us
    unnamed x1, local copies, waits for them, and re-layouts  1.87 us

profile of v1, /device:TPU:0, one launch (start us, length us, event | category | flops | bytes accessed | tf_op | source)
XLA Modules:
  0.0 38.0 jit_solution(1728243922501917762)
XLA Ops:
  0.0 36.2 %shard_map.82 = bf16[256,1024]{1,0:T(8,128)(2,1)} custom-call(bf16[3,256,1024]{2,1,0:T(8,128)(2,1)} %bitcast.2, f32[3,3,1024]{2,1,0:T(4,128)} %taps.1, bf16[64,4096]{1,0:T(8,128)(2,1)} %filt_hbm.1, f32[1,64]{1,0:T(1,128)} %bitcast.3, bf16[4,512,256]{2,1,0:T(8,128)(2,1)} %constant.8.clone.first_hbm, bf16[2,128,128]{2,1,0:T(8,128)(2,1)} %constant.9.clone.mid_hbm, ...), custom_call_target="tpu_custom_call" | custom-call | tf_op jit(solution)/shard_map/pallas_call | solution.py:410
  36.2 1.9 %copy.10 = bf16[256,1024]{1,0:T(8,128)(2,1)} copy(bf16[256,1024]{1,0:T(8,128)(2,1)} %shard_map.82) | data formatting | bytes 1048576

commit v2 on v1

--- a/solution.py
+++ b/solution.py
@@ -135,12 +135,9 @@
         query[tile] = q
         drive[tile] = d
 
-    loads[0].wait()
-    pl.loop(0, tiles // 2)(tile_features)
-
     pl.semaphore_wait(barrier, n - 1)
     m_copy = pltpu.make_async_remote_copy(
-        src_ref=proj.at[:, pl.ds(rows - mrows, mrows)],
+        src_ref=proj_hbm.at[:, pl.ds(rows - mrows, mrows)],
         dst_ref=margin,
         send_sem=m_send,
         recv_sem=m_recv,
@@ -151,8 +148,9 @@
     def _():
         m_copy.start()
 
-    early = 3 * tiles // 4
-    pl.loop(tiles // 2, early)(tile_features)
+    loads[0].wait()
+    early = tiles // 2
+    pl.loop(0, early, unroll=2)(tile_features)
 
     @pl.when(me > 0)
     def _():
@@ -261,9 +259,7 @@
     def group_rows(g, a=0):
         return pl.ds(pl.multiple_of(a * n2 + GROUP * g, GROUP), GROUP)
 
-    def filter_spectrum(k):
-        follow(k, 0, n // 2)
-
+    def filter_first(k):
         @pl.loop(0, groups, unroll=2)
         def _(g):
             wide = jnp.concatenate(
@@ -276,8 +272,7 @@
             res = jnp.dot(first[g], wide, preferred_element_type=F32)
             wide_f[:, :, group_rows(g), :] = res.astype(BF16).reshape(half, 2, GROUP, p * LANES)
 
-        follow(k, n // 2, n - 1)
-
+    def filter_last(k):
         def one(s, which):
             x = wide_f[s].reshape(2 * n2, p * LANES)
             z = jnp.dot(mid[which], x, preferred_element_type=F32)
@@ -352,8 +347,13 @@
         def _(step):
             send_long(k, offset(step)).start()
 
+    filter_first(0)
     for k in range(chunks):
-        filter_spectrum(k)
+        follow(k, 0, n // 2)
+        filter_last(k)
+        follow(k, n // 2, n - 1)
+        if k + 1 < chunks:
+            filter_first(k + 1)
         convolve(k)
 
     @pl.when(me < n - 1)

time: 38.2 us -> 39.1 us (1.024)
  Pallas kernels: 36.2 us -> 37 us
    pallas_call x1, Pallas kernels: 36.2 us -> 37 us  [body(): pl.pallas_call(functools.partial(kernel, n, chunks), out_shape=jax.ShapeD...]
where the time goes in v2:
time: 39.1 us; the launch traced here: 38.9 us
  Pallas kernels  37 us (95%)
  local copies, waits for them, and re-layouts  1.87 us (5%)
    pallas_call x1, Pallas kernels, body(): pl.pallas_call(functools.partial(kernel, n, chunks), out_shape=jax.ShapeD...  37 us
    unnamed x1, local copies, waits for them, and re-layouts  1.87 us

profile of v2, /device:TPU:0, one launch (start us, length us, event | category | flops | bytes accessed | tf_op | source)
XLA Modules:
  0.0 38.9 jit_solution(13750020343794831933)
XLA Ops:
  0.0 37.0 %shard_map.82 = bf16[256,1024]{1,0:T(8,128)(2,1)} custom-call(bf16[3,256,1024]{2,1,0:T(8,128)(2,1)} %bitcast.2, f32[3,3,1024]{2,1,0:T(4,128)} %taps.1, bf16[64,4096]{1,0:T(8,128)(2,1)} %filt_hbm.1, f32[1,64]{1,0:T(1,128)} %bitcast.3, bf16[4,512,256]{2,1,0:T(8,128)(2,1)} %constant.8.clone.first_hbm, bf16[2,128,128]{2,1,0:T(8,128)(2,1)} %constant.9.clone.mid_hbm, ...), custom_call_target="tpu_custom_call" | custom-call | tf_op jit(solution)/shard_map/pallas_call | solution.py:410
  37.1 1.9 %copy.10 = bf16[256,1024]{1,0:T(8,128)(2,1)} copy(bf16[256,1024]{1,0:T(8,128)(2,1)} %shard_map.82) | data formatting | bytes 1048576

commit v3 on v1

--- a/solution.py
+++ b/solution.py
@@ -13,6 +13,7 @@
 SUB = 8
 GROUP = 16
 MAX_PHASES = 4
+ROOM = 6 * 1024 * 1024
 F32 = jnp.float32
 BF16 = jnp.bfloat16
 
@@ -402,38 +403,40 @@
     half = n1 // 2
     tables = [jnp.asarray(t) for t in dft_tables(2 * total)]
     vmem = pl.BlockSpec(memory_space=pltpu.VMEM)
-    hbm = pl.BlockSpec(memory_space=pl.ANY)
+    hbm = pl.BlockSpec(memory_space=pltpu.HBM)
     sems = pltpu.SemaphoreType.DMA((chunks, n))
     blocks = pltpu.VMEM((chunks, n, rpd, LANES), BF16)
     flat = pltpu.VMEM((chunks, total, LANES), BF16)
     moved = jnp.transpose(projected, (1, 0, 2))
+    scratch = [
+        pltpu.VMEM(moved.shape, BF16),
+        pltpu.VMEM((filters.shape[0], LANES + length), BF16),
+        *[pltpu.VMEM(t.shape, BF16) for t in tables],
+        pltpu.VMEM((3, 16, chans), BF16),
+        pltpu.VMEM((chans // LANES, rows, LANES), F32),
+        pltpu.VMEM((chans // LANES, rows, LANES), F32),
+        blocks,
+        flat,
+        pltpu.VMEM((chunks, p, total, LANES), BF16),
+        pltpu.VMEM((half, 2, n2, p * LANES), BF16),
+        pltpu.VMEM((half, 2, n2, p * LANES), F32),
+        pltpu.VMEM((half, 2, n2, LANES), BF16),
+        flat,
+        blocks,
+        pltpu.SemaphoreType.DMA((6,)),
+        pltpu.SemaphoreType.DMA,
+        pltpu.SemaphoreType.DMA,
+        sems, sems, sems, sems,
+    ]
+    held = sum(math.prod(x.shape) * x.dtype.itemsize for x in scratch if getattr(x, "memory_space", None) == pltpu.VMEM)
     return pl.pallas_call(
         functools.partial(kernel, n, chunks),
         out_shape=jax.ShapeDtypeStruct((rows, chans), BF16),
         in_specs=[hbm, vmem, hbm, vmem] + [hbm] * 4,
         out_specs=vmem,
-        scratch_shapes=[
-            pltpu.VMEM(moved.shape, BF16),
-            pltpu.VMEM((filters.shape[0], LANES + length), BF16),
-            *[pltpu.VMEM(t.shape, BF16) for t in tables],
-            pltpu.VMEM((3, 16, chans), BF16),
-            pltpu.VMEM((chans // LANES, rows, LANES), F32),
-            pltpu.VMEM((chans // LANES, rows, LANES), F32),
-            blocks,
-            flat,
-            pltpu.VMEM((chunks, p, total, LANES), BF16),
-            pltpu.VMEM((half, 2, n2, p * LANES), BF16),
-            pltpu.VMEM((half, 2, n2, p * LANES), F32),
-            pltpu.VMEM((half, 2, n2, LANES), BF16),
-            flat,
-            blocks,
-            pltpu.SemaphoreType.DMA((6,)),
-            pltpu.SemaphoreType.DMA,
-            pltpu.SemaphoreType.DMA,
-            sems, sems, sems, sems,
-        ],
+        scratch_shapes=scratch,
         compiler_params=pltpu.CompilerParams(
-            collective_id=0, has_side_effects=True, vmem_limit_bytes=56 * 1024 * 1024
+            collective_id=0, has_side_effects=True, vmem_limit_bytes=held + ROOM
         ),
     )(moved, taps, filters, skip.reshape(1, lc), *tables)
 

time: 38.2 us -> 44.5 us (1.16)
  local copies, waits for them, and re-layouts: 1.87 us -> 8.82 us
  Pallas kernels: 36.2 us -> 35.2 us
    unnamed x1 -> x17, local copies, waits for them, and re-layouts: 1.87 us -> 8.82 us
    pallas_call x1, Pallas kernels: 36.2 us -> 35.2 us  [body(): pl.pallas_call(functools.partial(kernel, n, chunks), out_shape=jax.ShapeD...]
where the time goes in v3:
time: 44.5 us; the launch traced here: 44 us
  Pallas kernels  35.2 us (79%)
  local copies, waits for them, and re-layouts  8.82 us (20%)
    pallas_call x1, Pallas kernels, body(): pl.pallas_call(functools.partial(kernel, n, chunks), out_shape=jax.ShapeD...  35.2 us
    unnamed x17, local copies, waits for them, and re-layouts  8.82 us

profile of v3, /device:TPU:0, one launch (start us, length us, event | category | flops | bytes accessed | tf_op | source)
XLA Modules:
  0.0 44.0 jit_solution(4950534532035203215)
XLA Ops:
  0.0 0.0 copy-start
  0.0 1.4 %copy-done = bf16[256,3,1024]{2,0,1:T(8,128)(2,1)S(1)} copy-done((bf16[256,3,1024]{2,0,1:T(8,128)(2,1)S(1)}, bf16[256,3,1024]{2,0,1:T(8,128)(2,1)}, u32[]{:S(2)}) %copy-start) | copy-done | bytes 1572888
  1.4 0.0 copy-start.1
  1.4 1.2 %copy-done.1 = bf16[4,256,512]{2,1,0:T(8,128)(2,1)S(1)} copy-done((bf16[4,256,512]{2,1,0:T(8,128)(2,1)S(1)}, bf16[4,256,512]{2,1,0:T(8,128)(2,1)}, u32[]{:S(2)}) %copy-start.1) | copy-done | bytes 1048600
  2.6 0.0 copy-start.2
  2.6 1.2 %copy-done.2 = bf16[4,512,256]{2,1,0:T(8,128)(2,1)S(1)} copy-done((bf16[4,512,256]{2,1,0:T(8,128)(2,1)S(1)}, bf16[4,512,256]{2,1,0:T(8,128)(2,1)}, u32[]{:S(2)}) %copy-start.2) | copy-done | bytes 1048600
  3.9 0.0 copy-start.3
  3.9 1.0 %copy-done.3 = bf16[64,4096]{1,0:T(8,128)(2,1)S(1)} copy-done((bf16[64,4096]{1,0:T(8,128)(2,1)S(1)}, bf16[64,4096]{1,0:T(8,128)(2,1)}, u32[]{:S(2)}) %copy-start.3) | copy-done | bytes 524312
  4.9 0.0 copy-start.4
  4.9 0.8 %copy-done.4 = bf16[2,128,128]{2,1,0:T(8,128)(2,1)S(1)} copy-done((bf16[2,128,128]{2,1,0:T(8,128)(2,1)S(1)}, bf16[2,128,128]{2,1,0:T(8,128)(2,1)}, u32[]{:S(2)}) %copy-start.4) | copy-done | bytes 65560
  5.7 0.0 copy-start.5
  5.7 0.8 %copy-done.5 = bf16[2,128,128]{2,1,0:T(8,128)(2,1)S(1)} copy-done((bf16[2,128,128]{2,1,0:T(8,128)(2,1)S(1)}, bf16[2,128,128]{2,1,0:T(8,128)(2,1)}, u32[]{:S(2)}) %copy-start.5) | copy-done | bytes 65560
  6.6 0.0 copy-start.6
  6.6 0.8 %copy-done.6 = f32[3,3,1024]{2,1,0:T(4,128)S(1)} copy-done((f32[3,3,1024]{2,1,0:T(4,128)S(1)}, f32[3,3,1024]{2,1,0:T(4,128)}, u32[]{:S(2)}) %copy-start.6) | copy-done | bytes 36888
  7.4 0.0 copy-start.7
  7.4 0.7 %copy-done.7 = f32[64]{0:T(128)S(1)} copy-done((f32[64]{0:T(128)S(1)}, f32[64]{0:T(128)}, u32[]{:S(2)}) %copy-start.7) | copy-done | bytes 280
  8.0 35.2 %shard_map.82 = bf16[256,1024]{1,0:T(8,128)(2,1)S(1)} custom-call(bf16[3,256,1024]{2,1,0:T(8,128)(2,1)S(1)} %bitcast.2, f32[3,3,1024]{2,1,0:T(4,128)S(1)} %copy-done.6, bf16[64,4096]{1,0:T(8,128)(2,1)S(1)} %copy-done.3, f32[1,64]{1,0:T(1,128)S(1)} %bitcast.3, bf16[4,512,256]{2,1,0:T(8,128)(2,1)S(1)} %copy-done.2, bf16[2,128,128]{2,1,0:T(8,128)(2,1)S(1)} %copy-done.5, ...), custom_call_target="tpu_custom_call" | custom-call | tf_op jit(solution)/shard_map/pallas_call | solution.py:432
  43.2 0.8 %copy.10 = bf16[256,1024]{1,0:T(8,128)(2,1)} copy(bf16[256,1024]{1,0:T(8,128)(2,1)S(1)} %shard_map.82) | data formatting | bytes 1048576
Async XLA Ops:
  0.0 1.4 %copy-start = (bf16[256,3,1024]{2,0,1:T(8,128)(2,1)S(1)}, bf16[256,3,1024]{2,0,1:T(8,128)(2,1)}, u32[]{:S(2)}) copy-start(bf16[256,3,1024]{2,0,1:T(8,128)(2,1)} %param.8) | copy-start | bytes 4718596
  1.4 1.2 %copy-start.1 = (bf16[4,256,512]{2,1,0:T(8,128)(2,1)S(1)}, bf16[4,256,512]{2,1,0:T(8,128)(2,1)}, u32[]{:S(2)}) copy-start(bf16[4,256,512]{2,1,0:T(8,128)(2,1)} %constant.11.clone.last_hbm) | copy-start | bytes 3145732
  2.6 1.2 %copy-start.2 = (bf16[4,512,256]{2,1,0:T(8,128)(2,1)S(1)}, bf16[4,512,256]{2,1,0:T(8,128)(2,1)}, u32[]{:S(2)}) copy-start(bf16[4,512,256]{2,1,0:T(8,128)(2,1)} %constant.8.clone.first_hbm) | copy-start | bytes 3145732
  3.9 1.0 %copy-start.3 = (bf16[64,4096]{1,0:T(8,128)(2,1)S(1)}, bf16[64,4096]{1,0:T(8,128)(2,1)}, u32[]{:S(2)}) copy-start(bf16[64,4096]{1,0:T(8,128)(2,1)} %filt_hbm.1) | copy-start | bytes 1572868
  4.9 0.8 %copy-start.4 = (bf16[2,128,128]{2,1,0:T(8,128)(2,1)S(1)}, bf16[2,128,128]{2,1,0:T(8,128)(2,1)}, u32[]{:S(2)}) copy-start(bf16[2,128,128]{2,1,0:T(8,128)(2,1)} %constant.10.clone.back_hbm) | copy-start | bytes 196612
  5.7 0.8 %copy-start.5 = (bf16[2,128,128]{2,1,0:T(8,128)(2,1)S(1)}, bf16[2,128,128]{2,1,0:T(8,128)(2,1)}, u32[]{:S(2)}) copy-start(bf16[2,128,128]{2,1,0:T(8,128)(2,1)} %constant.9.clone.mid_hbm) | copy-start | bytes 196612
  6.6 0.8 %copy-start.6 = (f32[3,3,1024]{2,1,0:T(4,128)S(1)}, f32[3,3,1024]{2,1,0:T(4,128)}, u32[]{:S(2)}) copy-start(f32[3,3,1024]{2,1,0:T(4,128)} %taps.1) | copy-start | bytes 110596
  7.4 0.7 %copy-start.7 = (f32[64]{0:T(128)S(1)}, f32[64]{0:T(128)}, u32[]{:S(2)}) copy-start(f32[64]{0:T(128)} %param.11) | copy-start | bytes 772

commit v4 on v1

--- a/solution.py
+++ b/solution.py
@@ -226,13 +226,11 @@
     def offset(step):
         return lax.rem(n // 2 + step, n - 1) + 1
 
-    def follow(k, lo, hi):
-        if k + 1 < chunks:
-
-            @pl.loop(lo, hi)
-            def _(step):
-                send_drive(k, offset(step)).wait_send()
-                send_drive(k + 1, offset(step)).start()
+    for k in range(1, chunks):
+
+        @pl.loop(0, n - 1)
+        def _(step):
+            send_drive(k, offset(step)).start()
 
     loads[1].wait()
     seg = LANES // p
@@ -261,9 +259,7 @@
     def group_rows(g, a=0):
         return pl.ds(pl.multiple_of(a * n2 + GROUP * g, GROUP), GROUP)
 
-    def filter_spectrum(k):
-        follow(k, 0, n // 2)
-
+    def filter_first(k):
         @pl.loop(0, groups, unroll=2)
         def _(g):
             wide = jnp.concatenate(
@@ -276,8 +272,7 @@
             res = jnp.dot(first[g], wide, preferred_element_type=F32)
             wide_f[:, :, group_rows(g), :] = res.astype(BF16).reshape(half, 2, GROUP, p * LANES)
 
-        follow(k, n // 2, n - 1)
-
+    def filter_last(k):
         def one(s, which):
             x = wide_f[s].reshape(2 * n2, p * LANES)
             z = jnp.dot(mid[which], x, preferred_element_type=F32)
@@ -352,17 +347,22 @@
         def _(step):
             send_long(k, offset(step)).start()
 
+    filter_first(0)
     for k in range(chunks):
-        filter_spectrum(k)
+        filter_last(k)
+        if k + 1 < chunks:
+            filter_first(k + 1)
         convolve(k)
 
     @pl.when(me < n - 1)
     def _():
         m_copy.wait_send()
 
-    @pl.loop(1, n)
-    def _(i):
-        send_drive(chunks - 1, i).wait_send()
+    for k in range(chunks):
+
+        @pl.loop(1, n)
+        def _(i):
+            send_drive(k, i).wait_send()
 
     @pl.loop(0, tiles)
     def _(step):

time: 38.2 us -> 39.1 us (1.024)
  Pallas kernels: 36.2 us -> 37 us
    pallas_call x1, Pallas kernels: 36.2 us -> 37 us  [body(): pl.pallas_call(functools.partial(kernel, n, chunks), out_shape=jax.ShapeD...]
where the time goes in v4:
time: 39.1 us; the launch traced here: 38.9 us
  Pallas kernels  37 us (95%)
  local copies, waits for them, and re-layouts  1.87 us (5%)
    pallas_call x1, Pallas kernels, body(): pl.pallas_call(functools.partial(kernel, n, chunks), out_shape=jax.ShapeD...  37 us
    unnamed x1, local copies, waits for them, and re-layouts  1.87 us

profile of v4, /device:TPU:0, one launch (start us, length us, event | category | flops | bytes accessed | tf_op | source)
XLA Modules:
  0.0 38.9 jit_solution(17069376140964355557)
XLA Ops:
  0.0 37.0 %shard_map.82 = bf16[256,1024]{1,0:T(8,128)(2,1)} custom-call(bf16[3,256,1024]{2,1,0:T(8,128)(2,1)} %bitcast.2, f32[3,3,1024]{2,1,0:T(4,128)} %taps.1, bf16[64,4096]{1,0:T(8,128)(2,1)} %filt_hbm.1, f32[1,64]{1,0:T(1,128)} %bitcast.3, bf16[4,512,256]{2,1,0:T(8,128)(2,1)} %constant.8.clone.first_hbm, bf16[2,128,128]{2,1,0:T(8,128)(2,1)} %constant.9.clone.mid_hbm, ...), custom_call_target="tpu_custom_call" | custom-call | tf_op jit(solution)/shard_map/pallas_call | solution.py:410
  37.0 1.9 %copy.10 = bf16[256,1024]{1,0:T(8,128)(2,1)} copy(bf16[256,1024]{1,0:T(8,128)(2,1)} %shard_map.82) | data formatting | bytes 1048576

commit v5 on v1

--- a/solution.py
+++ b/solution.py
@@ -12,7 +12,7 @@
 LANES = 128
 SUB = 8
 GROUP = 16
-MAX_PHASES = 4
+MAX_PHASES = 2
 F32 = jnp.float32
 BF16 = jnp.bfloat16
 

time: 38.2 us -> 41.6 us (1.089)
  Pallas kernels: 36.2 us -> 39.5 us
    pallas_call x1, Pallas kernels: 36.2 us -> 39.5 us  [body(): pl.pallas_call(functools.partial(kernel, n, chunks), out_shape=jax.ShapeD...]
where the time goes in v5:
time: 41.6 us; the launch traced here: 41.4 us
  Pallas kernels  39.5 us (95%)
  local copies, waits for them, and re-layouts  1.87 us (4%)
    pallas_call x1, Pallas kernels, body(): pl.pallas_call(functools.partial(kernel, n, chunks), out_shape=jax.ShapeD...  39.5 us
    unnamed x1, local copies, waits for them, and re-layouts  1.87 us

profile of v5, /device:TPU:0, one launch (start us, length us, event | category | flops | bytes accessed | tf_op | source)
XLA Modules:
  0.0 41.4 jit_solution(15683491167164320701)
XLA Ops:
  0.0 39.5 %shard_map.82 = bf16[256,1024]{1,0:T(8,128)(2,1)} custom-call(bf16[3,256,1024]{2,1,0:T(8,128)(2,1)} %bitcast.2, f32[3,3,1024]{2,1,0:T(4,128)} %taps.1, bf16[64,4096]{1,0:T(8,128)(2,1)} %filt_hbm.1, f32[1,64]{1,0:T(1,128)} %bitcast.3, bf16[4,1024,512]{2,1,0:T(8,128)(2,1)} %constant.8.clone.first_hbm, bf16[2,128,128]{2,1,0:T(8,128)(2,1)} %constant.9.clone.mid_hbm, ...), custom_call_target="tpu_custom_call" | custom-call | tf_op jit(solution)/shard_map/pallas_call | solution.py:410
  39.5 1.9 %copy.10 = bf16[256,1024]{1,0:T(8,128)(2,1)} copy(bf16[256,1024]{1,0:T(8,128)(2,1)} %shard_map.82) | data formatting | bytes 1048576
